TPU v7x, 256 devices: a whole 4x4x8 slice. The times are simulated.
256 devices in a mesh: dp: 32 (over x, z), code: 8 (over y, core).
Axes of the slice: x: 4, y: 4, z: 8, core: 2. Of those that a mesh axis runs over, the one named last changes fastest.
Arguments:
- frames: bfloat16 [24576, 1024], P('dp')
- prototypes: bfloat16 [32768, 1024], P(('dp', 'code'))
Outputs:
- updated: bfloat16 [32768, 1024], P(('dp', 'code'))
- log_scale: float32 [24576], P('dp')
All inputs are finite; a program needn't handle non-finite values.
Results may differ from a plain program's by a relative error of at most 0.0095.
Values may be sent and summed in bfloat16 or wider, within the bound.
A program may use at most 192 MiB of HBM per device.

v0:
```python
import math

import jax
import jax.numpy as jnp
from jax import lax
from jax.sharding import PartitionSpec as P

K = 32768
ITERS = 3


sharpness_divisor = 0.05


def unit_rows(values):
    values_wide = values.astype(jnp.float32)
    return (
        values_wide
        * lax.rsqrt(jnp.mean(values_wide * values_wide, axis=1, keepdims=True) + 1e-06)
        / math.sqrt(values.shape[1])
    )


def per_device(frames, prototypes):
    count_of_rows = frames.shape[0]
    feat_width = frames.shape[1]
    own_rows = prototypes.shape[0]
    data_count = lax.axis_size("dp")
    total_frames = count_of_rows * data_count
    utterance_vector_length = unit_rows(frames).astype(jnp.bfloat16)
    proto_wide = unit_rows(prototypes)
    center_vector_length = proto_wide.astype(jnp.bfloat16)
    affinity_matrix = jnp.exp(
        lax.dot_general(
            utterance_vector_length,
            lax.all_gather(center_vector_length, "dp", axis=0, tiled=True),
            (((1,), (1,)), ((), ())),
            preferred_element_type=jnp.float32,
        )
        / sharpness_divisor
    )
    weight = jnp.full((count_of_rows,), 1.0 / total_frames, jnp.float32)
    balance = jnp.ones((affinity_matrix.shape[1],), jnp.float32)
    for iteration in range(ITERS):
        column = lax.psum(jnp.dot(weight, affinity_matrix, precision=lax.Precision.HIGHEST), "dp")
        balance = 1.0 / (K * column)
        row_total = lax.psum(
            jnp.dot(affinity_matrix, balance, precision=lax.Precision.HIGHEST), "code"
        )
        weight = 1.0 / (total_frames * row_total)
    partial_value = jnp.dot(weight, affinity_matrix, precision=lax.Precision.HIGHEST)
    start_at = lax.axis_index("dp") * own_rows
    global_weight_sum = lax.psum(partial_value, "dp")
    local_weight_share = lax.dynamic_slice_in_dim(global_weight_sum, start_at, own_rows)
    col_mass = (
        total_frames * lax.dynamic_slice_in_dim(balance, start_at, own_rows) * local_weight_share
    )
    assign = (total_frames * weight[:, None] * affinity_matrix * balance[None, :]).astype(
        jnp.bfloat16
    )
    pooled = lax.psum_scatter(
        lax.dot_general(
            assign,
            utterance_vector_length,
            (((0,), (0,)), ((), ())),
            preferred_element_type=jnp.float32,
        ).astype(jnp.bfloat16),
        "dp",
        scatter_dimension=0,
        tiled=True,
    ).astype(jnp.float32)
    log_scale = jnp.log(total_frames * weight)
    updated = (
        math.sqrt(feat_width) * (0.5 * proto_wide + 0.5 * pooled / col_mass[:, None])
    ).astype(jnp.bfloat16)
    return (updated, log_scale)


def solution(mesh):
    return jax.shard_map(
        per_device,
        mesh=mesh,
        in_specs=(P("dp", None), P(("dp", "code"), None)),
        out_specs=(P(("dp", "code"), None), P("dp")),
        check_vma=False,
    )
```

profile of v0, /device:TPU:1, one launch (start us, length us, event | category | flops | bytes accessed | tf_op | source)
XLA Modules:
  0.0 883.2 jit_solution(16271608029105534115)
XLA Ops:
  7.2 0.0 all-gather.2.cloned.1.call-start
  7.2 1.1 fusion.11
  8.3 1.8 fusion.10
  10.1 0.0 all-gather.2.cloned.1.call-update
  10.1 0.0 reduce-scatter.2.cloned.1.call-start
  10.2 1.8 fusion.2
  12.0 100.9 %all-gather.2.cloned.1.call-done = bf16[4096,1024]{1,0:T(8,128)(2,1)} async-done(((bf16[128,1024]{1,0:T(8,128)(2,1)}), bf16[4096,1024]{1,0:T(8,128)(2,1)}) %all-gather.2.cloned.1.call-update) | async-done | bytes 8388624 | tf_op jit(solution)/shard_map/all_gather | solution.py:36
  112.9 9.8 %multiply_exponential_fusion = f32[768,4096]{1,0:T(8,128)S(1)} fusion(bf16[4096,1024]{1,0:T(8,128)(2,1)} %all-gather.2.cloned.1.call-done, bf16[768,1024]{1,0:T(8,128)(2,1)} %param.2, f32[768]{0:T(1024)S(1)} %add_rsqrt_fusion), kind=kOutput, calls=%fused_computation.1 | convolution fusion | flops 6448742400 | bytes 22547456 | tf_op jit(solution)/shard_map/dot_general | solution.py:34
  122.7 0.0 copy-start
  122.7 4.6 copy-done
  127.3 6.0 fusion.14
  133.3 112.0 %psum.49 = f32[4096]{0:T(1024)S(1)} all-reduce(f32[4096]{0:T(1024)S(1)} %bitcast.27), channel_id=1, replica_groups=mesh['dp'=32,'code'=8] {'dp'}, use_global_device_ids=true, to_apply=%region_2.0 | all-reduce | flops 4096 | bytes 32768 | tf_op jit(solution)/shard_map/psum | solution.py:45
  245.3 13.3 %convolution_reduce_fusion.2 = f32[768]{0:T(1024)S(1)} fusion(f32[768,4096]{1,0:T(8,128)} %copy-done, f32[4096,1]{0,1:T(1,128)S(1)} %bitcast.23), kind=kOutput, calls=%fused_computation.12 | convolution fusion | flops 37748736 | bytes 12602368 | tf_op jit(solution)/shard_map/dot_general | solution.py:48
  258.6 40.3 %psum.50 = f32[768]{0:T(1024)S(1)} all-reduce(f32[768]{0:T(1024)S(1)} %convolution_reduce_fusion.2), channel_id=1, replica_groups=mesh['dp'=32,'code'=8] {'code'}, use_global_device_ids=true, to_apply=%region_3.0 | all-reduce | flops 768 | bytes 6144 | tf_op jit(solution)/shard_map/psum | solution.py:47
  298.9 8.5 fusion.20
  307.5 109.9 %psum.51 = f32[4096]{0:T(1024)S(1)} all-reduce(f32[4096]{0:T(1024)S(1)} %bitcast.24), channel_id=1, replica_groups=mesh['dp'=32,'code'=8] {'dp'}, use_global_device_ids=true, to_apply=%region_4.0 | all-reduce | flops 4096 | bytes 32768 | tf_op jit(solution)/shard_map/psum | solution.py:45
  417.4 13.3 %convolution_reduce_fusion.1 = f32[768]{0:T(1024)S(1)} fusion(f32[768,4096]{1,0:T(8,128)} %copy-done, f32[4096,1]{0,1:T(1,128)S(1)} %bitcast.25), kind=kOutput, calls=%fused_computation.11 | convolution fusion | flops 37748736 | bytes 12602368 | tf_op jit(solution)/shard_map/dot_general | solution.py:48
  430.7 40.4 %psum.52 = f32[768]{0:T(1024)S(1)} all-reduce(f32[768]{0:T(1024)S(1)} %convolution_reduce_fusion.1), channel_id=1, replica_groups=mesh['dp'=32,'code'=8] {'code'}, use_global_device_ids=true, to_apply=%region_5.0 | all-reduce | flops 768 | bytes 6144 | tf_op jit(solution)/shard_map/psum | solution.py:47
  471.1 8.5 fusion.21
  479.6 0.0 copy-start.2
  479.7 110.0 %psum.53 = f32[4096]{0:T(1024)S(1)} all-reduce(f32[4096]{0:T(1024)S(1)} %bitcast.26), channel_id=1, replica_groups=mesh['dp'=32,'code'=8] {'dp'}, use_global_device_ids=true, to_apply=%region_6.0 | all-reduce | flops 4096 | bytes 32768 | tf_op jit(solution)/shard_map/psum | solution.py:45
  589.7 13.3 %convolution_reduce_fusion = f32[768]{0:T(1024)S(1)} fusion(f32[768,4096]{1,0:T(8,128)} %copy-done, f32[4096,1]{0,1:T(1,128)S(1)} %bitcast.21), kind=kOutput, calls=%fused_computation.10 | convolution fusion | flops 37748736 | bytes 12602368 | tf_op jit(solution)/shard_map/dot_general | solution.py:48
  603.0 40.5 %psum.54 = f32[768]{0:T(1024)S(1)} all-reduce(f32[768]{0:T(1024)S(1)} %convolution_reduce_fusion), channel_id=1, replica_groups=mesh['dp'=32,'code'=8] {'code'}, use_global_device_ids=true, to_apply=%region_7.0 | all-reduce | flops 768 | bytes 6144 | tf_op jit(solution)/shard_map/psum | solution.py:47
  643.4 0.6 fusion.19
  644.1 0.0 copy-done.2
  644.1 14.3 %convolution_convert_fusion = bf16[4096,1024]{1,0:T(8,128)(2,1)} fusion(f32[768,4096]{1,0:T(8,128)} %copy-done, f32[4096]{0:T(1024)S(1)} %multiply_divide_fusion, f32[768]{0:T(1024)S(1)} %get-tuple-element.3, bf16[768,1024]{1,0:T(8,128)(2,1)S(1)} %copy-done.2, f32[768]{0:T(1024)S(1)} %add_rsqrt_fusion), kind=kOutput, calls=%fused_computation.2 | convolution fusion | flops 6459228160 | bytes 22566912 | tf_op jit(solution)/shard_map/dot_general | solution.py:62
  658.4 0.0 copy-start.1
  658.4 0.0 reduce-scatter.2.cloned.1.call-update
  658.4 8.6 fusion.22
  667.0 110.3 %psum.55 = f32[4096]{0:T(1024)S(1)} all-reduce(f32[4096]{0:T(1024)S(1)} %bitcast.22), channel_id=1, replica_groups=mesh['dp'=32,'code'=8] {'dp'}, use_global_device_ids=true, to_apply=%region_9.0 | all-reduce | flops 4096 | bytes 32768 | tf_op jit(solution)/shard_map/psum | solution.py:53
  777.3 0.1 dynamic-slice_multiply_fusion
  777.4 97.1 %reduce-scatter.2.cloned.1.call-done = bf16[128,1024]{1,0:T(8,128)(2,1)} async-done(((bf16[4096,1024]{1,0:T(8,128)(2,1)}), bf16[128,1024]{1,0:T(8,128)(2,1)}) %reduce-scatter.2.cloned.1.call-update) | async-done | bytes 262160 | tf_op jit(solution)/shard_map/reduce_scatter | solution.py:61
  874.5 0.0 copy-done.1
  874.5 1.9 fusion.9
  (10 shorter events, 0.1 us)
Async XLA Ops:
  7.2 105.7 %all-gather.2.cloned.1.call-start = ((), (), s32[]{:S(2)}) async-start(), calls=%async_computation.1 | async-start | bytes 8650752 | tf_op jit(solution)/shard_map/all_gather | solution.py:36
  10.1 864.4 %reduce-scatter.2.cloned.1.call-start = ((), (), s32[]{:S(2)}) async-start(), calls=%async_computation.2 | async-start | bytes 8650752 | tf_op jit(solution)/shard_map/reduce_scatter | solution.py:61
  122.7 4.6 copy-start
  479.6 164.4 %copy-start.2 = (bf16[768,1024]{1,0:T(8,128)(2,1)S(1)}, bf16[768,1024]{1,0:T(8,128)(2,1)}, u32[]{:S(2)}) copy-start(bf16[768,1024]{1,0:T(8,128)(2,1)} %param.2) | copy-start | bytes 4718596
  658.4 216.2 %copy-start.1 = (bf16[128,1024]{1,0:T(8,128)(2,1)S(1)}, bf16[128,1024]{1,0:T(8,128)(2,1)}, u32[]{:S(2)}) copy-start(bf16[128,1024]{1,0:T(8,128)(2,1)} %param.3) | copy-start | bytes 786436
Sparse Core Ops, SparseCore 0:
  11.2 101.6 all-gather.1
  658.5 215.9 reduce-scatter.1
where the time goes:
time: 887 us; the launch traced here: 883 us
  blocking collectives  563 us (63%)
  waiting for transfers between devices  198 us (22%)
  matrix products  95.6 us (11%)
  between operations  14.1 us (2%)
    psum x3, blocking collectives, per_device(): lax.psum(jnp.dot(weight, affinity_matrix, precision=lax.Precision.HIGHEST...  332 us
    psum x3, blocking collectives, per_device(): lax.psum(jnp.dot(affinity_matrix, balance, precision=lax.Precision.HIGHES...  121 us
    psum x1, blocking collectives, per_device(): global_weight_sum = lax.psum(partial_value, 'dp')  110 us
    all_gather x1, waiting for transfers between devices, per_device(): lax.all_gather(center_vector_length, 'dp', axis=0, tiled=True)  101 us
    reduce_scatter x1, waiting for transfers between devices, per_device(): lax.psum_scatter(lax.dot_general(assign, utterance_vector_length, (((0,),...  97.1 us
    dot_general x3, matrix products, per_device(): jnp.dot(affinity_matrix, balance, precision=lax.Precision.HIGHEST)  39.9 us
    dot_general x4, matrix products, per_device(): jnp.dot(weight, affinity_matrix, precision=lax.Precision.HIGHEST)  31.6 us
  transfers between devices with their start and end apart: 2, of which 2 were waited for; matrix products, arithmetic and copies ran while one was open for 1% of the time, Pallas kernels for 0%

commit v1 on v0

v1 whole, which is shorter than its diff:
```python
import functools

import jax
import jax.numpy as jnp
from jax import lax
from jax.experimental import pallas as pl
from jax.experimental.pallas import tpu as pltpu
from jax.sharding import PartitionSpec as P

MESH = pl.DeviceIdType.MESH
F32 = jnp.float32
BF16 = jnp.bfloat16

X, Y, Z = 4, 4, 8
D = 1024
K = 32768
F = 24576
ITERS = 3
FR = F // (X * Z)
PR = K // (X * Y * Z * 2)
NF = FR * X
NP = PR * Z
LT = NF // 128
QR = FR // 4
SR = QR // 2
HP = PR // 2

ORDER = (0, 1, 7, 2, 6, 3, 5, 4)
POS = {slot: position for position, slot in enumerate(ORDER)}


def place():
    dp = lax.axis_index("dp")
    code = lax.axis_index("code")
    return dp // Z, code // 2, lax.rem(dp, Z), lax.rem(code, 2)


def device(dx=0, dy=0, dz=0, dc=0):
    x, y, z, c = place()
    return {
        "dp": lax.rem(x + dx, X) * Z + lax.rem(z + dz, Z),
        "code": lax.rem(y + dy, Y) * 2 + lax.rem(c + dc, 2),
    }


PLANE = [(dx, dy) for dx in range(X) for dy in range(Y) if (dx, dy) != (0, 0)]


def unit_rows(values):
    wide = values.astype(F32)
    return wide * lax.rsqrt(jnp.sum(wide * wide, axis=1, keepdims=True) * (1.0 / D) + 1e-6) * (1.0 / 32.0)


def kernel(
    frames, protos, updated, log_scale,
    xn, pn, et, qb, pooled, cacc, bcol,
    csend, cslots, rpart, rsib, rslots, rwide, arow, brow,
    sbuf, rbuf,
    fx_recv, fy_recv, fs_recv, f_send, p_recv, p_send,
    c_recv, c_send, rs_recv, rs_send, r_recv, r_send, m_recv, m_send,
):
    x, y, z, c = place()
    barrier = pltpu.get_barrier_semaphore()
    partners = [dict(dz=e) for e in range(1, Z)] + [dict(dx=a, dy=b) for a, b in PLANE] + [dict(dc=1)]
    for where in partners:
        pl.semaphore_signal(barrier, inc=1, device_id=device(**where), device_id_type=MESH)

    pn[0:PR, :] = unit_rows(protos[...]).astype(BF16)

    def norm_body(i, _):
        rows = pl.ds(pl.multiple_of(i * 64, 64), 64)
        xn[rows, :] = unit_rows(frames[rows, :]).astype(BF16)
        return 0

    lax.fori_loop(0, FR // 64, norm_body, 0)
    pl.semaphore_wait(barrier, len(partners))

    def send(src, dst, send_sem, recv_sem, **where):
        pltpu.make_async_remote_copy(
            src_ref=src, dst_ref=dst, send_sem=send_sem, recv_sem=recv_sem,
            device_id=device(**where), device_id_type=MESH,
        ).start()

    def wait(ref, sem):
        pltpu.make_async_copy(ref, ref, sem).wait()

    parity = lax.rem(y, 2)
    mine = parity * 2 + c
    other = (1 - parity) * 2 + c

    def frame_rows(slot, quarter, sub):
        start = slot * FR + quarter * QR + sub * SR
        return xn.at[pl.ds(pl.multiple_of(start, 32), SR), :]

    def x_send(slot_from, slot_to, sub, dx):
        send(frame_rows(slot_from, mine, sub), frame_rows(slot_to, mine, sub), f_send, fx_recv.at[slot_to, sub], dx=dx)

    def y_send(slot, sub):
        up = (slot == 3) == (sub == 1)
        send(frame_rows(slot, mine, sub), frame_rows(slot, mine, sub), f_send, fy_recv.at[slot, sub], dy=1 if up else 3)

    def sib_send(slot, quarter, sub):
        send(frame_rows(slot, quarter, sub), frame_rows(slot, quarter, sub), f_send, fs_recv.at[slot], dc=1)

    def x_arrival(slot, sub):
        ref = frame_rows(slot, mine, sub)
        wait(ref, fx_recv.at[slot, sub])
        if slot == 1 and sub == 0:
            x_send(1, 2, 0, 3)
        if slot == 3 and sub == 1:
            x_send(3, 2, 1, 1)
        y_send(slot, sub)
        sib_send(slot, mine, sub)

    def y_arrival(slot, sub):
        wait(frame_rows(slot, other, sub), fy_recv.at[slot, sub])
        sib_send(slot, other, sub)

    def frames_done(slot):
        wait(xn.at[0 : 4 * SR, :], fs_recv.at[slot])

    def proto_rows(slot, sub):
        start = POS[slot] * PR + sub * HP
        return pn.at[start : start + HP, :]

    def p_hop(slot_from, slot_to, sub, dz):
        send(proto_rows(slot_from, sub), proto_rows(slot_to, sub), p_send, p_recv.at[slot_to, sub], dz=dz)

    def p_arrival(slot, sub):
        wait(proto_rows(slot, sub), p_recv.at[slot, sub])
        if slot in (1, 2) or (slot == 3 and sub == 0):
            p_hop(slot, slot + 1, sub, Z - 1)
        if slot in (7, 6) or (slot == 5 and sub == 1):
            p_hop(slot, slot - 1, sub, 1)

    for sub in range(2):
        x_send(0, 1, sub, 3)
        x_send(0, 3, sub, 1)
        p_hop(0, 1, sub, Z - 1)
        p_hop(0, 7, 1 - sub, 1)

    def score(row0, count, slot, first):
        rows = pl.ds(row0, count)
        columns = slice(slot * FR, (slot + 1) * FR)
        product = lax.dot_general(
            pn[rows, :], xn[columns, :], (((1,), (1,)), ((), ())), preferred_element_type=F32
        )
        value = jnp.exp(product * 20.0)
        et[rows, columns] = value
        part = value[:, 0:128]
        for j in range(1, FR // 128):
            part = part + value[:, j * 128 : (j + 1) * 128]
        if first:
            cacc[rows, :] = part
        else:
            cacc[rows, :] = cacc[rows, :] + part

    score(0, PR, 0, True)
    p_arrival(1, 0)
    p_arrival(7, 1)
    x_arrival(1, 0)
    x_arrival(3, 0)
    p_arrival(1, 1)
    p_arrival(7, 0)
    score(PR, 2 * PR, 0, True)
    x_arrival(1, 1)
    x_arrival(3, 1)
    p_arrival(2, 0)
    p_arrival(6, 1)
    y_arrival(1, 0)
    y_arrival(3, 0)
    p_arrival(2, 1)
    p_arrival(6, 0)
    score(3 * PR, 2 * PR, 0, True)
    x_arrival(2, 0)
    x_arrival(2, 1)
    p_arrival(3, 0)
    p_arrival(5, 1)
    y_arrival(1, 1)
    y_arrival(3, 1)
    frames_done(1)
    frames_done(3)
    for slot in (1, 3):
        score(0, PR, slot, False)
        score(PR, 2 * PR, slot, False)
    p_arrival(3, 1)
    p_arrival(5, 0)
    for slot in (1, 3):
        score(3 * PR, 2 * PR, slot, False)
    y_arrival(2, 0)
    y_arrival(2, 1)
    for slot in (0, 1, 3):
        score(5 * PR, 2 * PR, slot, slot == 0)
    p_arrival(4, 0)
    p_arrival(4, 1)
    for slot in (0, 1, 3):
        score(7 * PR, PR, slot, slot == 0)
    frames_done(2)

    def score_body(i, _):
        score(pl.multiple_of(i * 256, 256), 256, 2, False)
        return 0

    lax.fori_loop(0, NP // 256, score_body, 0)

    eye = lax.broadcasted_iota(jnp.int32, (128, 128), 0) == lax.broadcasted_iota(jnp.int32, (128, 128), 1)

    def column_start(k):
        for p in range(Z):
            column = jnp.sum(cacc[p * PR : (p + 1) * PR, :], axis=1, keepdims=True)
            csend[k, ORDER[p] : ORDER[p] + 1, :] = jnp.sum(jnp.where(eye, column, 0.0), axis=0, keepdims=True)
        for e in range(1, Z):
            send(csend.at[k], cslots.at[k, e - 1], c_send.at[k], c_recv.at[k], dz=e)

    def column_total(k):
        wait(cslots.at[k], c_recv.at[k])
        total = csend[k]
        for e in range(1, Z):
            total = total + pltpu.roll(cslots[k, e - 1], Z - e, 0)
        return total

    def to_column(row):
        return jnp.sum(jnp.where(eye, row, 0.0), axis=1, keepdims=True)

    def row_pass(k):
        def body(i, acc):
            acc = list(acc)
            for g in range(8):
                rows = pl.ds(pl.multiple_of(i * 64 + g * 8, 8), 8)
                weight = bcol[rows, :]
                for j in range(LT):
                    acc[j] = acc[j] + et[rows, j * 128 : (j + 1) * 128] * weight
            return tuple(acc)

        acc = lax.fori_loop(0, NP // 64, body, tuple(jnp.zeros((8, 128), F32) for _ in range(LT)))
        for j in range(LT):
            rpart[k, j : j + 1, :] = jnp.sum(acc[j], axis=0, keepdims=True)

    def row_total(k):
        send(rpart.at[k], rsib.at[k], rs_send.at[k], rs_recv.at[k], dc=1)
        wait(rsib.at[k], rs_recv.at[k])
        rslots[k, y] = rpart[k] + rsib[k]
        for dx, dy in PLANE:
            send(rslots.at[k, y], rslots.at[k, dx * Y + y], r_send.at[k], r_recv.at[k], dx=dx, dy=dy)
        wait(rslots.at[k, 0 : X * Y - 1], r_recv.at[k])
        total = None
        for dx in range(X):
            slots = [rslots[k, dx * Y + dy] for dy in range(Y)]
            part = (slots[0] + slots[1]) + (slots[2] + slots[3])
            if dx == 0:
                total = part
            else:
                rwide[0:LT, :] = part
                rwide[LT : 2 * LT, :] = part
                shift = dx * (FR // 128)
                total = total + rwide[shift : shift + LT, :]
        return total

    def column_pass():
        weights = [jnp.broadcast_to(arow[j : j + 1, :], (8, 128)) for j in range(LT)]

        def body(i, _):
            for g in range(8):
                rows = pl.ds(pl.multiple_of(i * 64 + g * 8, 8), 8)
                acc = [None] * 4
                for j in range(LT):
                    term = et[rows, j * 128 : (j + 1) * 128] * weights[j]
                    acc[j % 4] = term if acc[j % 4] is None else acc[j % 4] + term
                cacc[rows, :] = (acc[0] + acc[1]) + (acc[2] + acc[3])
            return 0

        lax.fori_loop(0, NP // 64, body, 0)

    def last_pass():
        weights = [jnp.broadcast_to(arow[j : j + 1, :] * float(F), (16, 128)) for j in range(LT)]

        def body(i, _):
            for g in range(4):
                rows = pl.ds(pl.multiple_of(i * 64 + g * 16, 16), 16)
                acc = [None] * 2
                for j in range(LT):
                    columns = slice(j * 128, (j + 1) * 128)
                    term = et[rows, columns] * weights[j]
                    qb[rows, columns] = term.astype(BF16)
                    acc[j % 2] = term if acc[j % 2] is None else acc[j % 2] + term
                cacc[rows, :] = acc[0] + acc[1]
            return 0

        lax.fori_loop(0, NP // 64, body, 0)

    for k in range(ITERS):
        column_start(k)
        total = column_total(k)
        if k == 0:
            total = total * (1.0 / F)
        brow[...] = 1.0 / (float(K) * total)
        for p in range(Z):
            bcol[p * PR : (p + 1) * PR, :] = jnp.broadcast_to(
                to_column(brow[ORDER[p] : ORDER[p] + 1, :]), (PR, 128)
            )
        row_pass(k)
        arow[...] = 1.0 / (float(F) * row_total(k))
        if k < ITERS - 1:
            column_pass()
    last_pass()
    column_start(ITERS)
    log_scale[...] = jnp.log(float(F) * arow[0:8, :])

    def pool(position, count):
        rows = slice(position * PR, (position + count) * PR)

        def body(n, _):
            columns = pl.ds(pl.multiple_of(n * 256, 256), 256)
            pooled[rows, columns] = jnp.dot(qb[rows, :], xn[:, columns], preferred_element_type=F32)
            return 0

        lax.fori_loop(0, D // 256, body, 0)

    def hop(way, step, sub):
        slot = 4 - step if way == 0 else 4 + step
        start = POS[slot] * PR + sub * HP
        value = pooled[start : start + HP, :]
        if step > 1 or (step == 1 and sub == way):
            before = slice((step - 1) * PR + sub * HP, (step - 1) * PR + (sub + 1) * HP)
            wait(rbuf.at[way, before, :], m_recv.at[way, step - 1, sub])
            value = value + rbuf[way, before, :].astype(F32)
        half = slice(step * PR + sub * HP, step * PR + (sub + 1) * HP)
        sbuf[way, half, :] = value.astype(BF16)
        send(
            sbuf.at[way, half, :], rbuf.at[way, half, :],
            m_send.at[way], m_recv.at[way, step, sub], dz=1 if way == 0 else Z - 1,
        )

    pool(POS[4], 1)
    hop(0, 0, 0)
    hop(1, 0, 1)
    pool(POS[3], 2)
    hop(0, 1, 1)
    hop(1, 1, 0)
    pool(POS[2], 2)
    hop(0, 1, 0)
    hop(1, 1, 1)
    pool(POS[1], 2)
    for step in (2, 3):
        if step == 3:
            pool(0, 1)
        for turn in range(2):
            hop(0, step, 1 - turn)
            hop(1, step, turn)

    mass = brow[0:1, :] * column_total(ITERS)[0:1, :]
    scale_column = to_column(brow[0:1, :] / mass)
    wide = unit_rows(protos[...])
    for turn in range(2):
        for way in range(2):
            sub = 1 - turn if way == 0 else turn
            half = slice(3 * PR + sub * HP, 3 * PR + (sub + 1) * HP)
            wait(rbuf.at[way, half, :], m_recv.at[way, 3, sub])
    last = slice(3 * PR, 4 * PR)
    own = pooled[0:PR, :] + rbuf[0, last, :].astype(F32) + rbuf[1, last, :].astype(F32)
    updated[...] = (32.0 * (0.5 * wide + 0.5 * (own * scale_column))).astype(BF16)

    wait(xn.at[0 : 24 * SR, :], f_send)
    wait(pn.at[0 : 14 * HP, :], p_send)
    for k in range(ITERS + 1):
        wait(cslots.at[k], c_send.at[k])
    for k in range(ITERS):
        wait(rsib.at[k], rs_send.at[k])
        wait(rslots.at[k, 0 : X * Y - 1], r_send.at[k])
    for way in range(2):
        wait(sbuf.at[way, 0 : 7 * HP, :], m_send.at[way])


def per_device(frames, prototypes):
    vmem = pl.BlockSpec(memory_space=pltpu.VMEM)
    dma = pltpu.SemaphoreType.DMA
    updated, log_scale = pl.pallas_call(
        kernel,
        out_shape=(jax.ShapeDtypeStruct((PR, D), BF16), jax.ShapeDtypeStruct((8, 128), F32)),
        in_specs=[vmem, vmem],
        out_specs=(vmem, vmem),
        scratch_shapes=[
            pltpu.VMEM((NF, D), BF16),
            pltpu.VMEM((NP, D), BF16),
            pltpu.VMEM((NP, NF), F32),
            pltpu.VMEM((NP, NF), BF16),
            pltpu.VMEM((NP, D), F32),
            pltpu.VMEM((NP, 128), F32),
            pltpu.VMEM((NP, 128), F32),
            pltpu.VMEM((ITERS + 1, Z, 128), F32),
            pltpu.VMEM((ITERS + 1, Z - 1, Z, 128), F32),
            pltpu.VMEM((ITERS, LT, 128), F32),
            pltpu.VMEM((ITERS, LT, 128), F32),
            pltpu.VMEM((ITERS, X * Y, LT, 128), F32),
            pltpu.VMEM((2 * LT, 128), F32),
            pltpu.VMEM((LT, 128), F32),
            pltpu.VMEM((Z, 128), F32),
            pltpu.VMEM((2, 4 * PR, D), BF16),
            pltpu.VMEM((2, 4 * PR, D), BF16),
            dma((4, 2)), dma((4, 2)), dma((4,)), dma,
            dma((Z, 2)), dma,
            dma((ITERS + 1,)), dma((ITERS + 1,)),
            dma((ITERS,)), dma((ITERS,)), dma((ITERS,)), dma((ITERS,)),
            dma((2, 4, 2)), dma((2,)),
        ],
        compiler_params=pltpu.CompilerParams(
            collective_id=0, has_side_effects=True, vmem_limit_bytes=56 * 2**20
        ),
    )(frames, prototypes)
    return updated, log_scale[0 : FR // 128].reshape(FR)


def solution(mesh):
    return jax.shard_map(
        per_device,
        mesh=mesh,
        in_specs=(P("dp", None), P(("dp", "code"), None)),
        out_specs=(P(("dp", "code"), None), P("dp")),
        check_vma=False,
    )
```

time: 887 us -> 109 us (0.12)
  blocking collectives: 563 us -> 0 us
  waiting for transfers between devices: 198 us -> 0 us
  Pallas kernels: 0 us -> 105 us
  matrix products: 95.6 us -> 0 us
  between operations: 14.1 us -> 0.64 us
    psum x7 -> x0, blocking collectives: 563 us -> none  [the longest x3 332 us: per_device(): lax.psum(jnp.dot(weight, affinity_matrix, precision=lax.Precision.HIGHEST...]
    pallas_call x0 -> x1, Pallas kernels: none -> 105 us  [per_device(): pl.pallas_call(kernel, out_shape=(jax.ShapeDtypeStruct((PR, D), BF16), ja...]
    all_gather x1 -> x0, waiting for transfers between devices: 101 us -> none  [per_device(): lax.all_gather(center_vector_length, 'dp', axis=0, tiled=True)]
    reduce_scatter x1 -> x0, waiting for transfers between devices: 97.1 us -> none  [per_device(): lax.psum_scatter(lax.dot_general(assign, utterance_vector_length, (((0,),...]
    dot_general x9 -> x0, matrix products: 95.6 us -> none  [the longest x3 39.9 us: per_device(): jnp.dot(affinity_matrix, balance, precision=lax.Precision.HIGHEST)]
  transfers between devices with their start and end apart: 2 -> 0, of which waited for: 2 -> 0; matrix products, arithmetic and copies ran while one was open for 1% -> 0% of each run, Pallas kernels for 0% -> 0%
where the time goes in v1:
time: 109 us
  Pallas kernels  105 us (96%)
  local copies, waits for them, and re-layouts  2.95 us (3%)
    pallas_call x1, Pallas kernels, per_device(): pl.pallas_call(kernel, out_shape=(jax.ShapeDtypeStruct((PR, D), BF16), ja...  105 us

profile of v1, /device:TPU:1, one launch (start us, length us, event | category | flops | bytes accessed | tf_op | source)
XLA Modules:
  0.0 108.9 jit_solution(3093436394290911199)
XLA Ops:
  0.6 105.3 %shard_map.41 = (bf16[128,1024]{1,0:T(8,128)(2,1)}, f32[8,128]{1,0:T(8,128)}) custom-call(bf16[768,1024]{1,0:T(8,128)(2,1)} %frames.1, bf16[128,1024]{1,0:T(8,128)(2,1)} %protos.1), custom_call_target="tpu_custom_call" | custom-call | tf_op jit(solution)/shard_map/pallas_call | solution.py:377
  105.9 1.3 %slice_bitcast_fusion = f32[768]{0:T(1024)} fusion(f32[8,128]{1,0:T(8,128)} %get-tuple-element.5), kind=kLoop, calls=%fused_computation | loop fusion | bytes 6144 | tf_op jit(solution)/shard_map/reshape | solution.py:410
  107.2 1.7 %copy.5 = bf16[128,1024]{1,0:T(8,128)(2,1)} copy(bf16[128,1024]{1,0:T(8,128)(2,1)} %get-tuple-element.8) | data formatting | bytes 524288

commit v2 on v1

v2 whole, which is shorter than its diff:
```python
import functools

import jax
import jax.numpy as jnp
from jax import lax
from jax.experimental import pallas as pl
from jax.experimental.pallas import tpu as pltpu
from jax.sharding import PartitionSpec as P

MESH = pl.DeviceIdType.MESH
F32 = jnp.float32
BF16 = jnp.bfloat16

X, Y, Z = 4, 4, 8
D = 1024
K = 32768
F = 24576
ITERS = 3
FR = F // (X * Z)
PR = K // (X * Y * Z * 2)
NF = FR * X
NP = PR * Z
LT = NF // 128
QR = FR // 4
SUBS = 4
SR = QR // SUBS
HP = PR // SUBS
CW = D // SUBS
RC = LT // 8

ORDER = (0, 1, 7, 2, 6, 3, 5, 4)
POS = {slot: position for position, slot in enumerate(ORDER)}
TURNS = {0: (2, 3, 0, 1), 1: (0, 1, 2, 3)}
NEAR = [dict(dx=1), dict(dx=X - 1), dict(dy=1), dict(dy=Y - 1), dict(dz=1), dict(dz=Z - 1), dict(dc=1)]
ROUNDS = 3


def place():
    dp = lax.axis_index("dp")
    code = lax.axis_index("code")
    return dp // Z, code // 2, lax.rem(dp, Z), lax.rem(code, 2)


def device(dx=0, dy=0, dz=0, dc=0):
    x, y, z, c = place()
    return {
        "dp": lax.rem(x + dx, X) * Z + lax.rem(z + dz, Z),
        "code": lax.rem(y + dy, Y) * 2 + lax.rem(c + dc, 2),
    }


def ring(step, size):
    return min(step, size - step)


PLANE = sorted(
    [(dx, dy) for dx in range(X) for dy in range(Y) if (dx, dy) != (0, 0)],
    key=lambda d: -ring(d[0], X) - ring(d[1], Y),
)
LINE = sorted(range(1, Z), key=lambda e: -ring(e, Z))


def unit_rows(values):
    wide = values.astype(F32)
    return wide * lax.rsqrt(jnp.sum(wide * wide, axis=1, keepdims=True) * (1.0 / D) + 1e-6) * (1.0 / 32.0)


def kernel(
    frames_hbm, protos_hbm, updated, log_scale,
    frames, protos, xn, pn, et, qb, pooled, cacc, bcol,
    csend, cslots, rpart, rsib, rslots, rwide, arow, brow, base,
    sbuf, rbuf,
    in_sem, hop_sem,
    fx_recv, fy_recv, fs_recv, f_send, p_recv, p_send,
    c_recv, c_send, rs_recv, rs_send, r_recv, r_send, m_recv, m_send,
):
    x, y, z, c = place()
    protos_in = pltpu.make_async_copy(protos_hbm, protos, in_sem.at[0])
    frames_in = pltpu.make_async_copy(frames_hbm, frames, in_sem.at[1])
    protos_in.start()
    frames_in.start()
    barrier = pltpu.get_barrier_semaphore()
    for where in NEAR:
        pl.semaphore_signal(barrier, inc=1, device_id=device(**where), device_id_type=MESH)

    protos_in.wait()
    base[...] = unit_rows(protos[...])
    pn[0:PR, :] = base[...].astype(BF16)
    frames_in.wait()

    def norm_body(i, _):
        rows = pl.ds(pl.multiple_of(i * 64, 64), 64)
        xn[rows, :] = unit_rows(frames[rows, :]).astype(BF16)
        return 0

    lax.fori_loop(0, FR // 64, norm_body, 0)
    pl.semaphore_wait(barrier, len(NEAR))

    def tell(r):
        for where in NEAR:
            pl.semaphore_signal(hop_sem.at[r], inc=1, device_id=device(**where), device_id_type=MESH)

    def hear(r):
        pl.semaphore_wait(hop_sem.at[r], len(NEAR))

    def send(src, dst, send_sem, recv_sem, **where):
        pltpu.make_async_remote_copy(
            src_ref=src, dst_ref=dst, send_sem=send_sem, recv_sem=recv_sem,
            device_id=device(**where), device_id_type=MESH,
        ).start()

    def wait(ref, sem):
        pltpu.make_async_copy(ref, ref, sem).wait()

    parity = lax.rem(y, 2)
    mine = parity * 2 + c
    other = (1 - parity) * 2 + c

    def frame_rows(slot, quarter, sub):
        start = slot * FR + quarter * QR + sub * SR
        return xn.at[pl.ds(pl.multiple_of(start, 16), SR), :]

    def x_send(slot_from, slot_to, sub, dx):
        send(frame_rows(slot_from, mine, sub), frame_rows(slot_to, mine, sub), f_send, fx_recv.at[slot_to, sub], dx=dx)

    def y_send(slot, sub, up):
        send(frame_rows(slot, mine, sub), frame_rows(slot, mine, sub), f_send, fy_recv.at[slot, sub], dy=1 if up else Y - 1)

    def sib_send(slot, quarter, sub):
        send(frame_rows(slot, quarter, sub), frame_rows(slot, quarter, sub), f_send, fs_recv.at[slot], dc=1)

    def x_arrival(turn):
        if turn < SUBS:
            pieces = [(1, TURNS[1][turn], turn % 2 == 0), (3, TURNS[0][turn], turn % 2 == 1)]
        else:
            pieces = [(2, TURNS[1][turn - SUBS], True), (2, TURNS[0][turn - SUBS], False)]
        for slot, sub, up in pieces:
            wait(frame_rows(slot, mine, sub), fx_recv.at[slot, sub])
            if turn < 2:
                if slot == 1:
                    x_send(1, 2, sub, X - 1)
                else:
                    x_send(3, 2, sub, 1)
            y_send(slot, sub, up)
            sib_send(slot, mine, sub)

    def y_arrival(turn):
        if turn < SUBS:
            pieces = [(1, TURNS[1][turn]), (3, TURNS[0][turn])]
        else:
            pieces = [(2, TURNS[1][turn - SUBS]), (2, TURNS[0][turn - SUBS])]
        for slot, sub in pieces:
            wait(frame_rows(slot, other, sub), fy_recv.at[slot, sub])
            sib_send(slot, other, sub)

    def frames_done(slot):
        wait(xn.at[0 : 2 * SUBS * SR, :], fs_recv.at[slot])

    def proto_rows(slot, sub):
        start = POS[slot] * PR + sub * HP
        return pn.at[start : start + HP, :]

    def p_hop(slot_from, slot_to, sub, dz):
        send(proto_rows(slot_from, sub), proto_rows(slot_to, sub), p_send, p_recv.at[slot_to, sub], dz=dz)

    def p_arrival(hop, turn):
        if hop == 4:
            for way in range(2):
                sub = TURNS[way][turn]
                wait(proto_rows(4, sub), p_recv.at[4, sub])
            return
        for way, slot in ((1, hop), (0, Z - hop)):
            sub = TURNS[way][turn]
            wait(proto_rows(slot, sub), p_recv.at[slot, sub])
            if hop < 3 or turn < 2:
                p_hop(slot, slot + 1 if way == 1 else slot - 1, sub, Z - 1 if way == 1 else 1)

    for turn in range(SUBS):
        x_send(0, 1, TURNS[1][turn], X - 1)
        x_send(0, 3, TURNS[0][turn], 1)
        p_hop(0, 1, TURNS[1][turn], Z - 1)
        p_hop(0, 7, TURNS[0][turn], 1)
    tell(0)

    def score(position, count, column, width):
        rows = slice(position * PR, (position + count) * PR)
        columns = slice(column, column + width)
        product = lax.dot_general(
            pn[rows, :], xn[columns, :], (((1,), (1,)), ((), ())), preferred_element_type=F32
        )
        value = jnp.exp(product * 20.0)
        et[rows, columns] = value
        part = value[:, 0:128]
        for j in range(1, width // 128):
            part = part + value[:, j * 128 : (j + 1) * 128]
        if column == 0:
            cacc[rows, :] = part
        else:
            cacc[rows, :] = cacc[rows, :] + part

    score(0, 1, 0, FR)
    p_arrival(1, 0)
    x_arrival(0)
    p_arrival(1, 1)
    hear(0)
    tell(1)
    p_arrival(1, 2)
    x_arrival(1)
    p_arrival(1, 3)
    score(1, 2, 0, FR)
    x_arrival(2)
    p_arrival(2, 0)
    y_arrival(0)
    hear(1)
    tell(2)
    p_arrival(2, 1)
    x_arrival(3)
    y_arrival(1)
    p_arrival(2, 2)
    x_arrival(4)
    p_arrival(2, 3)
    y_arrival(2)
    score(3, 2, 0, FR)
    p_arrival(3, 0)
    x_arrival(5)
    y_arrival(3)
    hear(2)
    p_arrival(3, 1)
    frames_done(1)
    frames_done(3)
    score(0, 5, FR, 256)
    score(0, 5, FR + 256, 256)
    p_arrival(3, 2)
    y_arrival(4)
    score(0, 5, FR + 512, 256)
    score(0, 5, 3 * FR, 256)
    p_arrival(3, 3)
    y_arrival(5)
    score(0, 5, 3 * FR + 256, 256)
    score(0, 5, 3 * FR + 512, 256)
    for slot in (0, 1, 3):
        score(5, 2, slot * FR, FR)
    frames_done(2)
    for n in range(3):
        score(0, 7, 2 * FR + n * 256, 256)
    p_arrival(4, 0)
    p_arrival(4, 1)
    for slot in range(X):
        score(7, 1, slot * FR, FR)

    eye = lax.broadcasted_iota(jnp.int32, (128, 128), 0) == lax.broadcasted_iota(jnp.int32, (128, 128), 1)

    def column_start(k):
        for p in range(Z):
            column = jnp.sum(cacc[p * PR : (p + 1) * PR, :], axis=1, keepdims=True)
            csend[k, ORDER[p] : ORDER[p] + 1, :] = jnp.sum(jnp.where(eye, column, 0.0), axis=0, keepdims=True)
        for e in LINE:
            send(csend.at[k], cslots.at[k, e - 1], c_send.at[k], c_recv.at[k], dz=e)

    def column_total(k):
        wait(cslots.at[k], c_recv.at[k])
        total = csend[k]
        for e in range(1, Z):
            total = total + pltpu.roll(cslots[k, e - 1], Z - e, 0)
        return total

    def to_column(row):
        return jnp.sum(jnp.where(eye, row, 0.0), axis=1, keepdims=True)

    def row_pass(k):
        for j in range(RC):
            def body(i, acc):
                acc = list(acc)
                for g in range(8):
                    rows = pl.ds(pl.multiple_of(i * 64 + g * 8, 8), 8)
                    weight = bcol[rows, :]
                    for t in range(8):
                        at = (g % 2) * 8 + t
                        acc[at] = acc[at] + et[rows, (j * 8 + t) * 128 : (j * 8 + t + 1) * 128] * weight
                return tuple(acc)

            acc = lax.fori_loop(0, NP // 64, body, tuple(jnp.zeros((8, 128), F32) for _ in range(16)))
            for t in range(8):
                rpart[k, j, t : t + 1, :] = jnp.sum(acc[t] + acc[8 + t], axis=0, keepdims=True)
            send(rpart.at[k, j], rsib.at[k, j], rs_send.at[k, j], rs_recv.at[k, j], dc=1)

    def row_total(k):
        for j in range(RC):
            wait(rsib.at[k, j], rs_recv.at[k, j])
            rslots[k, j, y] = rpart[k, j] + rsib[k, j]
            for dx, dy in PLANE:
                send(
                    rslots.at[k, j, y], rslots.at[k, j, dx * Y + y], r_send.at[k, j], r_recv.at[k, j], dx=dx, dy=dy
                )
        for j in range(RC):
            wait(rslots.at[k, j, 0 : X * Y - 1], r_recv.at[k, j])
            for dx in range(X):
                slots = [rslots[k, j, dx * Y + dy] for dy in range(Y)]
                part = (slots[0] + slots[1]) + (slots[2] + slots[3])
                rwide[dx, j * 8 : (j + 1) * 8, :] = part
                if dx > 0:
                    rwide[dx, LT + j * 8 : LT + (j + 1) * 8, :] = part
        total = rwide[0, 0:LT, :]
        for dx in range(1, X):
            shift = dx * (FR // 128)
            total = total + rwide[dx, shift : shift + LT, :]
        return total

    def column_pass():
        weights = [jnp.broadcast_to(arow[j : j + 1, :], (8, 128)) for j in range(LT)]

        def body(i, _):
            for g in range(8):
                rows = pl.ds(pl.multiple_of(i * 64 + g * 8, 8), 8)
                acc = [None] * 4
                for j in range(LT):
                    term = et[rows, j * 128 : (j + 1) * 128] * weights[j]
                    acc[j % 4] = term if acc[j % 4] is None else acc[j % 4] + term
                cacc[rows, :] = (acc[0] + acc[1]) + (acc[2] + acc[3])
            return 0

        lax.fori_loop(0, NP // 64, body, 0)

    def last_pass(position, count):
        weights = [jnp.broadcast_to(arow[j : j + 1, :] * float(F), (16, 128)) for j in range(LT)]

        def body(i, _):
            for g in range(4):
                rows = pl.ds(pl.multiple_of(position * PR + i * 64 + g * 16, 16), 16)
                acc = [None] * 2
                for j in range(LT):
                    columns = slice(j * 128, (j + 1) * 128)
                    term = et[rows, columns] * weights[j]
                    qb[rows, columns] = term.astype(BF16)
                    acc[j % 2] = term if acc[j % 2] is None else acc[j % 2] + term
                cacc[rows, :] = acc[0] + acc[1]
            return 0

        lax.fori_loop(0, count * PR // 64, body, 0)

    for k in range(ITERS):
        column_start(k)
        total = column_total(k)
        if k == 0:
            total = total * (1.0 / F)
        brow[...] = 1.0 / (float(K) * total)
        for p in range(Z):
            bcol[p * PR : (p + 1) * PR, :] = jnp.broadcast_to(
                to_column(brow[ORDER[p] : ORDER[p] + 1, :]), (PR, 128)
            )
        row_pass(k)
        arow[...] = 1.0 / (float(F) * row_total(k))
        if k < ITERS - 1:
            column_pass()

    def pool(position, count, sub):
        rows = slice(position * PR, (position + count) * PR)
        columns = slice(sub * CW, (sub + 1) * CW)
        pooled[rows, columns] = jnp.dot(qb[rows, :], xn[:, columns], preferred_element_type=F32)

    def hop(way, step, sub):
        slot = 4 - step if way == 0 else 4 + step
        start = POS[slot] * PR
        value = pooled[start : start + PR, sub * CW : (sub + 1) * CW]
        if step > 1 or (step == 1 and sub in TURNS[1 - way][0:2]):
            wait(rbuf.at[way, (step - 1) * SUBS + sub], m_recv.at[way, step - 1, sub])
            value = value + rbuf[way, (step - 1) * SUBS + sub].astype(F32)
        sbuf[way, step * SUBS + sub] = value.astype(BF16)
        send(
            sbuf.at[way, step * SUBS + sub], rbuf.at[way, step * SUBS + sub],
            m_send.at[way], m_recv.at[way, step, sub], dz=1 if way == 0 else Z - 1,
        )

    last_pass(POS[4], 1)
    for turn in (2, 3):
        for way in range(2):
            sub = TURNS[way][turn]
            pool(POS[4], 1, sub)
            hop(way, 0, sub)
    last_pass(POS[3], 2)
    for turn in range(2):
        for way in range(2):
            sub = TURNS[way][turn]
            pool(POS[3], 2, sub)
            hop(way, 1, sub)
    last_pass(0, 5)
    hop(0, 1, TURNS[0][2])
    hop(1, 1, TURNS[1][2])
    column_start(ITERS)
    log_scale[...] = jnp.log(float(F) * arow[0:8, :])
    hop(0, 1, TURNS[0][3])
    hop(1, 1, TURNS[1][3])
    for step in (2, 3):
        for turn in range(2):
            for way in range(2):
                sub = TURNS[way][turn]
                pool(POS[4 - step], 2, sub)
                hop(way, step, sub)
        for turn in range(2, 4):
            hop(0, step, TURNS[0][turn])
            hop(1, step, TURNS[1][turn])
    for sub in range(SUBS):
        pool(0, 1, sub)

    mass = brow[0:1, :] * column_total(ITERS)[0:1, :]
    scale_column = to_column(brow[0:1, :] / mass)
    for sub in (2, 0, 3, 1):
        columns = slice(sub * CW, (sub + 1) * CW)
        own = pooled[0:PR, columns]
        for way in range(2):
            wait(rbuf.at[way, 3 * SUBS + sub], m_recv.at[way, 3, sub])
            own = own + rbuf[way, 3 * SUBS + sub].astype(F32)
        updated[:, columns] = (32.0 * (0.5 * base[:, columns] + 0.5 * (own * scale_column))).astype(BF16)

    wait(xn.at[0 : 12 * SUBS * SR, :], f_send)
    wait(pn.at[0 : 7 * SUBS * HP, :], p_send)
    for k in range(ITERS + 1):
        wait(cslots.at[k], c_send.at[k])
    for k in range(ITERS):
        for j in range(RC):
            wait(rsib.at[k, j], rs_send.at[k, j])
            wait(rslots.at[k, j, 0 : X * Y - 1], r_send.at[k, j])
    for way in range(2):
        wait(sbuf.at[way, 0 : 14], m_send.at[way])


def per_device(frames, prototypes):
    hbm = pl.BlockSpec(memory_space=pl.ANY)
    vmem = pl.BlockSpec(memory_space=pltpu.VMEM)
    dma = pltpu.SemaphoreType.DMA
    updated, log_scale = pl.pallas_call(
        kernel,
        out_shape=(jax.ShapeDtypeStruct((PR, D), BF16), jax.ShapeDtypeStruct((8, 128), F32)),
        in_specs=[hbm, hbm],
        out_specs=(vmem, vmem),
        scratch_shapes=[
            pltpu.VMEM((FR, D), BF16),
            pltpu.VMEM((PR, D), BF16),
            pltpu.VMEM((NF, D), BF16),
            pltpu.VMEM((NP, D), BF16),
            pltpu.VMEM((NP, NF), F32),
            pltpu.VMEM((NP, NF), BF16),
            pltpu.VMEM((NP, D), F32),
            pltpu.VMEM((NP, 128), F32),
            pltpu.VMEM((NP, 128), F32),
            pltpu.VMEM((ITERS + 1, Z, 128), F32),
            pltpu.VMEM((ITERS + 1, Z - 1, Z, 128), F32),
            pltpu.VMEM((ITERS, RC, 8, 128), F32),
            pltpu.VMEM((ITERS, RC, 8, 128), F32),
            pltpu.VMEM((ITERS, RC, X * Y, 8, 128), F32),
            pltpu.VMEM((X, 2 * LT, 128), F32),
            pltpu.VMEM((LT, 128), F32),
            pltpu.VMEM((Z, 128), F32),
            pltpu.VMEM((PR, D), F32),
            pltpu.VMEM((2, 4 * SUBS, PR, CW), BF16),
            pltpu.VMEM((2, 4 * SUBS, PR, CW), BF16),
            dma((2,)), pltpu.SemaphoreType.REGULAR((ROUNDS,)),
            dma((X, SUBS)), dma((X, SUBS)), dma((X,)), dma,
            dma((Z, SUBS)), dma,
            dma((ITERS + 1,)), dma((ITERS + 1,)),
            dma((ITERS, RC)), dma((ITERS, RC)), dma((ITERS, RC)), dma((ITERS, RC)),
            dma((2, 4, SUBS)), dma((2,)),
        ],
        compiler_params=pltpu.CompilerParams(
            collective_id=0, has_side_effects=True, vmem_limit_bytes=56 * 2**20
        ),
    )(frames, prototypes)
    return updated, log_scale[0 : FR // 128].reshape(FR)


def solution(mesh):
    return jax.shard_map(
        per_device,
        mesh=mesh,
        in_specs=(P("dp", None), P(("dp", "code"), None)),
        out_specs=(P(("dp", "code"), None), P("dp")),
        check_vma=False,
    )
```

time: 109 us -> 106 us (0.972)
  Pallas kernels: 105 us -> 102 us
    pallas_call x1, Pallas kernels: 105 us -> 102 us  [per_device(): pl.pallas_call(kernel, out_shape=(jax.ShapeDtypeStruct((PR, D), BF16), ja...]
where the time goes in v2:
time: 106 us
  Pallas kernels  102 us (96%)
  local copies, waits for them, and re-layouts  2.95 us (3%)
    pallas_call x1, Pallas kernels, per_device(): pl.pallas_call(kernel, out_shape=(jax.ShapeDtypeStruct((PR, D), BF16), ja...  102 us

profile of v2, /device:TPU:1, one launch (start us, length us, event | category | flops | bytes accessed | tf_op | source)
XLA Modules:
  0.0 105.5 jit_solution(11139746585456663248)
XLA Ops:
  0.6 102.0 %shard_map.41 = (bf16[128,1024]{1,0:T(8,128)(2,1)}, f32[8,128]{1,0:T(8,128)}) custom-call(bf16[768,1024]{1,0:T(8,128)(2,1)} %frames_hbm.1, bf16[128,1024]{1,0:T(8,128)(2,1)} %protos_hbm.1), custom_call_target="tpu_custom_call" | custom-call | tf_op jit(solution)/shard_map/pallas_call | solution.py:431
  102.6 1.3 %slice_bitcast_fusion = f32[768]{0:T(1024)} fusion(f32[8,128]{1,0:T(8,128)} %get-tuple-element.5), kind=kLoop, calls=%fused_computation | loop fusion | bytes 6144 | tf_op jit(solution)/shard_map/reshape | solution.py:468
  103.9 1.7 %copy.5 = bf16[128,1024]{1,0:T(8,128)(2,1)} copy(bf16[128,1024]{1,0:T(8,128)(2,1)} %get-tuple-element.8) | data formatting | bytes 524288

commit v3 on v2

--- a/solution.py
+++ b/solution.py
@@ -30,9 +30,10 @@
 
 ORDER = (0, 1, 7, 2, 6, 3, 5, 4)
 POS = {slot: position for position, slot in enumerate(ORDER)}
+SUBPOS = (0, 2, 1, 3)
 TURNS = {0: (2, 3, 0, 1), 1: (0, 1, 2, 3)}
 NEAR = [dict(dx=1), dict(dx=X - 1), dict(dy=1), dict(dy=Y - 1), dict(dz=1), dict(dz=Z - 1), dict(dc=1)]
-ROUNDS = 3
+ROUNDS = 4
 
 
 def place():
@@ -41,12 +42,17 @@
     return dp // Z, code // 2, lax.rem(dp, Z), lax.rem(code, 2)
 
 
-def device(dx=0, dy=0, dz=0, dc=0):
+def neighbours():
     x, y, z, c = place()
-    return {
-        "dp": lax.rem(x + dx, X) * Z + lax.rem(z + dz, Z),
-        "code": lax.rem(y + dy, Y) * 2 + lax.rem(c + dc, 2),
-    }
+    xs = [lax.rem(x + d, X) * Z for d in range(X)]
+    ys = [lax.rem(y + d, Y) * 2 for d in range(Y)]
+    zs = [lax.rem(z + d, Z) for d in range(Z)]
+    cs = [c, 1 - c]
+
+    def device(dx=0, dy=0, dz=0, dc=0):
+        return {"dp": xs[dx] + zs[dz], "code": ys[dy] + cs[dc]}
+
+    return device
 
 
 def ring(step, size):
@@ -54,7 +60,7 @@
 
 
 PLANE = sorted(
-    [(dx, dy) for dx in range(X) for dy in range(Y) if (dx, dy) != (0, 0)],
+    [(dx, dy, dc) for dx in range(X) for dy in range(Y) for dc in range(2) if (dx, dy, dc) != (0, 0, 0)],
     key=lambda d: -ring(d[0], X) - ring(d[1], Y),
 )
 LINE = sorted(range(1, Z), key=lambda e: -ring(e, Z))
@@ -68,13 +74,14 @@
 def kernel(
     frames_hbm, protos_hbm, updated, log_scale,
     frames, protos, xn, pn, et, qb, pooled, cacc, bcol,
-    csend, cslots, rpart, rsib, rslots, rwide, arow, brow, base,
+    csend, cslots, rslots, rwide, arow, brow, base,
     sbuf, rbuf,
     in_sem, hop_sem,
     fx_recv, fy_recv, fs_recv, f_send, p_recv, p_send,
-    c_recv, c_send, rs_recv, rs_send, r_recv, r_send, m_recv, m_send,
+    c_recv, c_send, r_recv, r_send, m_recv, m_send,
 ):
     x, y, z, c = place()
+    device = neighbours()
     protos_in = pltpu.make_async_copy(protos_hbm, protos, in_sem.at[0])
     frames_in = pltpu.make_async_copy(frames_hbm, frames, in_sem.at[1])
     protos_in.start()
@@ -117,7 +124,7 @@
     other = (1 - parity) * 2 + c
 
     def frame_rows(slot, quarter, sub):
-        start = slot * FR + quarter * QR + sub * SR
+        start = slot * FR + SUBPOS[sub] * QR + quarter * SR
         return xn.at[pl.ds(pl.multiple_of(start, 16), SR), :]
 
     def x_send(slot_from, slot_to, sub, dx):
@@ -127,7 +134,7 @@
         send(frame_rows(slot, mine, sub), frame_rows(slot, mine, sub), f_send, fy_recv.at[slot, sub], dy=1 if up else Y - 1)
 
     def sib_send(slot, quarter, sub):
-        send(frame_rows(slot, quarter, sub), frame_rows(slot, quarter, sub), f_send, fs_recv.at[slot], dc=1)
+        send(frame_rows(slot, quarter, sub), frame_rows(slot, quarter, sub), f_send, fs_recv.at[slot, sub % 2 if slot == 2 else 0], dc=1)
 
     def x_arrival(turn):
         if turn < SUBS:
@@ -153,8 +160,9 @@
             wait(frame_rows(slot, other, sub), fy_recv.at[slot, sub])
             sib_send(slot, other, sub)
 
-    def frames_done(slot):
-        wait(xn.at[0 : 2 * SUBS * SR, :], fs_recv.at[slot])
+    def frames_done(slot, half=0):
+        count = SUBS if slot == 2 else 2 * SUBS
+        wait(xn.at[0 : count * SR, :], fs_recv.at[slot, half])
 
     def proto_rows(slot, sub):
         start = POS[slot] * PR + sub * HP
@@ -225,6 +233,7 @@
     x_arrival(5)
     y_arrival(3)
     hear(2)
+    tell(3)
     p_arrival(3, 1)
     frames_done(1)
     frames_done(3)
@@ -236,17 +245,20 @@
     score(0, 5, 3 * FR, 256)
     p_arrival(3, 3)
     y_arrival(5)
+    hear(3)
     score(0, 5, 3 * FR + 256, 256)
     score(0, 5, 3 * FR + 512, 256)
     for slot in (0, 1, 3):
         score(5, 2, slot * FR, FR)
-    frames_done(2)
-    for n in range(3):
-        score(0, 7, 2 * FR + n * 256, 256)
     p_arrival(4, 0)
     p_arrival(4, 1)
-    for slot in range(X):
+    for slot in (0, 1, 3):
         score(7, 1, slot * FR, FR)
+    frames_done(2, 0)
+    score(0, 8, 2 * FR, 256)
+    frames_done(2, 1)
+    score(0, 8, 2 * FR + 256, 256)
+    score(0, 8, 2 * FR + 512, 256)
 
     eye = lax.broadcasted_iota(jnp.int32, (128, 128), 0) == lax.broadcasted_iota(jnp.int32, (128, 128), 1)
 
@@ -281,22 +293,21 @@
 
             acc = lax.fori_loop(0, NP // 64, body, tuple(jnp.zeros((8, 128), F32) for _ in range(16)))
             for t in range(8):
-                rpart[k, j, t : t + 1, :] = jnp.sum(acc[t] + acc[8 + t], axis=0, keepdims=True)
-            send(rpart.at[k, j], rsib.at[k, j], rs_send.at[k, j], rs_recv.at[k, j], dc=1)
+                rslots[k, j, y * 2 + c, t : t + 1, :] = jnp.sum(acc[t] + acc[8 + t], axis=0, keepdims=True)
+            for dx, dy, dc in PLANE:
+                send(
+                    rslots.at[k, j, y * 2 + c], rslots.at[k, j, dx * Y * 2 + y * 2 + c],
+                    r_send.at[k, j], r_recv.at[k, j], dx=dx, dy=dy, dc=dc,
+                )
 
     def row_total(k):
         for j in range(RC):
-            wait(rsib.at[k, j], rs_recv.at[k, j])
-            rslots[k, j, y] = rpart[k, j] + rsib[k, j]
-            for dx, dy in PLANE:
-                send(
-                    rslots.at[k, j, y], rslots.at[k, j, dx * Y + y], r_send.at[k, j], r_recv.at[k, j], dx=dx, dy=dy
-                )
-        for j in range(RC):
-            wait(rslots.at[k, j, 0 : X * Y - 1], r_recv.at[k, j])
+            wait(rslots.at[k, j, 0 : X * Y * 2 - 1], r_recv.at[k, j])
             for dx in range(X):
-                slots = [rslots[k, j, dx * Y + dy] for dy in range(Y)]
-                part = (slots[0] + slots[1]) + (slots[2] + slots[3])
+                slots = [rslots[k, j, dx * Y * 2 + i] for i in range(Y * 2)]
+                while len(slots) > 1:
+                    slots = [slots[i] + slots[i + 1] for i in range(0, len(slots), 2)]
+                part = slots[0]
                 rwide[dx, j * 8 : (j + 1) * 8, :] = part
                 if dx > 0:
                     rwide[dx, LT + j * 8 : LT + (j + 1) * 8, :] = part
@@ -383,22 +394,23 @@
             sub = TURNS[way][turn]
             pool(POS[3], 2, sub)
             hop(way, 1, sub)
-    last_pass(0, 5)
-    hop(0, 1, TURNS[0][2])
-    hop(1, 1, TURNS[1][2])
-    column_start(ITERS)
-    log_scale[...] = jnp.log(float(F) * arow[0:8, :])
-    hop(0, 1, TURNS[0][3])
-    hop(1, 1, TURNS[1][3])
-    for step in (2, 3):
+    for step in (1, 2):
+        last_pass(POS[3 - step], 2)
+        for turn in range(2):
+            for way in range(2):
+                hop(way, step, TURNS[way][turn + 2])
+            if turn == 0 and step == 2:
+                last_pass(0, 1)
+                column_start(ITERS)
+                log_scale[...] = jnp.log(float(F) * arow[0:8, :])
         for turn in range(2):
             for way in range(2):
                 sub = TURNS[way][turn]
-                pool(POS[4 - step], 2, sub)
-                hop(way, step, sub)
-        for turn in range(2, 4):
-            hop(0, step, TURNS[0][turn])
-            hop(1, step, TURNS[1][turn])
+                pool(POS[3 - step], 2, sub)
+                hop(way, step + 1, sub)
+    for turn in range(2):
+        hop(0, 3, TURNS[0][turn + 2])
+        hop(1, 3, TURNS[1][turn + 2])
     for sub in range(SUBS):
         pool(0, 1, sub)
 
@@ -418,10 +430,15 @@
         wait(cslots.at[k], c_send.at[k])
     for k in range(ITERS):
         for j in range(RC):
-            wait(rsib.at[k, j], rs_send.at[k, j])
-            wait(rslots.at[k, j, 0 : X * Y - 1], r_send.at[k, j])
+            wait(rslots.at[k, j, 0 : X * Y * 2 - 1], r_send.at[k, j])
     for way in range(2):
         wait(sbuf.at[way, 0 : 14], m_send.at[way])
+
+
+def finish(updated, log_scale, updated_out, log_scale_out):
+    updated_out[...] = updated[...]
+    for j in range(FR // 128):
+        log_scale_out[j * 128 : (j + 1) * 128] = log_scale[j, :]
 
 
 def per_device(frames, prototypes):
@@ -445,9 +462,7 @@
             pltpu.VMEM((NP, 128), F32),
             pltpu.VMEM((ITERS + 1, Z, 128), F32),
             pltpu.VMEM((ITERS + 1, Z - 1, Z, 128), F32),
-            pltpu.VMEM((ITERS, RC, 8, 128), F32),
-            pltpu.VMEM((ITERS, RC, 8, 128), F32),
-            pltpu.VMEM((ITERS, RC, X * Y, 8, 128), F32),
+            pltpu.VMEM((ITERS, RC, X * Y * 2, 8, 128), F32),
             pltpu.VMEM((X, 2 * LT, 128), F32),
             pltpu.VMEM((LT, 128), F32),
             pltpu.VMEM((Z, 128), F32),
@@ -455,17 +470,22 @@
             pltpu.VMEM((2, 4 * SUBS, PR, CW), BF16),
             pltpu.VMEM((2, 4 * SUBS, PR, CW), BF16),
             dma((2,)), pltpu.SemaphoreType.REGULAR((ROUNDS,)),
-            dma((X, SUBS)), dma((X, SUBS)), dma((X,)), dma,
+            dma((X, SUBS)), dma((X, SUBS)), dma((X, 2)), dma,
             dma((Z, SUBS)), dma,
             dma((ITERS + 1,)), dma((ITERS + 1,)),
-            dma((ITERS, RC)), dma((ITERS, RC)), dma((ITERS, RC)), dma((ITERS, RC)),
+            dma((ITERS, RC)), dma((ITERS, RC)),
             dma((2, 4, SUBS)), dma((2,)),
         ],
         compiler_params=pltpu.CompilerParams(
             collective_id=0, has_side_effects=True, vmem_limit_bytes=56 * 2**20
         ),
     )(frames, prototypes)
-    return updated, log_scale[0 : FR // 128].reshape(FR)
+    return pl.pallas_call(
+        finish,
+        out_shape=(jax.ShapeDtypeStruct((PR, D), BF16), jax.ShapeDtypeStruct((FR,), F32)),
+        in_specs=[vmem, vmem],
+        out_specs=(vmem, vmem),
+    )(updated, log_scale)
 
 
 def solution(mesh):

time: 106 us -> 104 us (0.981)
  local copies, waits for them, and re-layouts: 2.95 us -> 0 us
    pallas_call x0 -> x1, Pallas kernels: none -> 1.68 us  [per_device(): pl.pallas_call(finish, out_shape=(jax.ShapeDtypeStruct((PR, D), BF16), ja...]
    unnamed x1 -> x0, local copies, waits for them, and re-layouts: 1.67 us -> none
    reshape x1 -> x0, local copies, waits for them, and re-layouts: 1.28 us -> none  [per_device(): return (updated, log_scale[0:FR // 128].reshape(FR))]
where the time goes in v3:
time: 104 us
  Pallas kernels  103 us (99%)
    pallas_call x1, Pallas kernels, per_device(): pl.pallas_call(kernel, out_shape=(jax.ShapeDtypeStruct((PR, D), BF16), ja...  102 us

profile of v3, /device:TPU:1, one launch (start us, length us, event | category | flops | bytes accessed | tf_op | source)
XLA Modules:
  0.0 104.0 jit_solution(7571127342872006457)
XLA Ops:
  0.6 101.7 %shard_map.41 = (bf16[128,1024]{1,0:T(8,128)(2,1)}, f32[8,128]{1,0:T(8,128)}) custom-call(bf16[768,1024]{1,0:T(8,128)(2,1)} %frames_hbm.1, bf16[128,1024]{1,0:T(8,128)(2,1)} %protos_hbm.1), custom_call_target="tpu_custom_call" | custom-call | tf_op jit(solution)/shard_map/pallas_call | solution.py:448
  102.3 1.7 %shard_map.42 = (bf16[128,1024]{1,0:T(8,128)(2,1)}, f32[768]{0:T(1024)}) custom-call(bf16[128,1024]{1,0:T(8,128)(2,1)} %get-tuple-element.4.updated, f32[8,128]{1,0:T(8,128)} %get-tuple-element.5.log_scale), custom_call_target="tpu_custom_call" | custom-call | tf_op jit(solution)/shard_map/pallas_call | solution.py:483

commit v4 on v3

--- a/solution.py
+++ b/solution.py
@@ -248,14 +248,15 @@
     hear(3)
     score(0, 5, 3 * FR + 256, 256)
     score(0, 5, 3 * FR + 512, 256)
-    for slot in (0, 1, 3):
-        score(5, 2, slot * FR, FR)
+    score(5, 2, 0, FR)
+    frames_done(2, 0)
+    score(0, 5, 2 * FR, 256)
     p_arrival(4, 0)
     p_arrival(4, 1)
-    for slot in (0, 1, 3):
-        score(7, 1, slot * FR, FR)
-    frames_done(2, 0)
-    score(0, 8, 2 * FR, 256)
+    score(7, 1, 0, FR)
+    for slot in (1, 3):
+        score(5, 3, slot * FR, FR)
+    score(5, 3, 2 * FR, 256)
     frames_done(2, 1)
     score(0, 8, 2 * FR + 256, 256)
     score(0, 8, 2 * FR + 512, 256)

time: 104 us -> 103 us (level)
  no operation moved by 1% of the time
where the time goes in v4:
time: 103 us
  Pallas kernels  103 us (100%)
    pallas_call x1, Pallas kernels, per_device(): pl.pallas_call(kernel, out_shape=(jax.ShapeDtypeStruct((PR, D), BF16), ja...  101 us

profile of v4, /device:TPU:1, one launch (start us, length us, event | category | flops | bytes accessed | tf_op | source)
XLA Modules:
  0.0 103.3 jit_solution(17201754483846656143)
XLA Ops:
  0.6 101.0 %shard_map.41 = (bf16[128,1024]{1,0:T(8,128)(2,1)}, f32[8,128]{1,0:T(8,128)}) custom-call(bf16[768,1024]{1,0:T(8,128)(2,1)} %frames_hbm.1, bf16[128,1024]{1,0:T(8,128)(2,1)} %protos_hbm.1), custom_call_target="tpu_custom_call" | custom-call | tf_op jit(solution)/shard_map/pallas_call | solution.py:449
  101.7 1.7 %shard_map.42 = (bf16[128,1024]{1,0:T(8,128)(2,1)}, f32[768]{0:T(1024)}) custom-call(bf16[128,1024]{1,0:T(8,128)(2,1)} %get-tuple-element.4.updated, f32[8,128]{1,0:T(8,128)} %get-tuple-element.5.log_scale), custom_call_target="tpu_custom_call" | custom-call | tf_op jit(solution)/shard_map/pallas_call | solution.py:484
